TPU v7x, 32 devices: a whole 2x2x4 slice. The times are simulated.
32 devices in a mesh: req: 8 (over y, x, core), blk: 4 (over z).
Axes of the slice: x: 2, y: 2, z: 4, core: 2. Of those that a mesh axis runs over, the one named last changes fastest.
Arguments:
- x_img: bfloat16 [8, 1024, 1536], P('req', 'blk'), may hold values from -0.3 to 0.3
- x_txt: bfloat16 [8, 154, 1536], P('req'), may hold values from -6 to 6
- modulation: float32 [8, 7, 1536], P('req'), may hold values from -8 to 8
- w_img: bfloat16 [1536, 2304], P(None, 'req'), may hold values from -0.375 to 0.375
- w_txt: bfloat16 [1536, 1536], P(None, 'req'), may hold values from -0.15625 to 0.15625
- w_out: bfloat16 [768, 1536], P('req'), may hold values from -0.21875 to 0.21875
- w_final: bfloat16 [1536, 64], replicated, may hold values from -0.15625 to 0.15625
- lengths: int32 [8], P('req'), may hold values from 16 to 154, as said below
- block_mask: int32 [8, 4, 4], P('req', 'blk'), may hold values from 0 to 1, as said below
- timestep: int32 [8], P('req'), may hold values from 0 to 27
- latent: float32 [8, 16, 32, 128], P('req', None, 'blk'), may hold values from -6 to 6
- conv_w: bfloat16 [512, 144], replicated, may hold values from -0.5 to 0.5
Outputs:
- velocity: float32 [8, 16, 32, 128], P('req', None, 'blk')
- latent_next: float32 [8, 16, 32, 128], P('req', None, 'blk')
- features: bfloat16 [8, 512, 32, 128], P('req', None, 'blk')
Inputs may be any that keep to these rules, and one draw needn't show every extreme that they name: Text keys from position lengths[r] on are padding; some request uses all 154 text tokens. Every tile may attend to its own keys: block_mask[r, t, t] = 1.
All inputs are finite; a program needn't handle non-finite values.
Results may differ from a plain program's by a relative error of at most 0.0063.
Values may be sent and summed in bfloat16 or wider, within the bound.
A program may use at most 192 MiB of HBM per device.

v0:
```python
import jax
import jax.numpy as jnp
from jax import lax
from jax.sharding import PartitionSpec as P

HD = 64
GRIDW = 64
PATCH = 2
LATC = 16
NSTEPS = 28
NORM_EPS = 1e-06
SHIFT_FACTOR = 3.0
LATENT_SCALE = 1.5305
LATENT_SHIFT = 0.0609
NEG_LARGE = -1e30
SCORE_SCALE = 0.125


def with_halo(block, sides, width):
    for axis, dim in sides:
        count = lax.axis_size(axis)
        forward = [(i, i + 1) for i in range(count - 1)]
        backward = [(target, source) for source, target in forward]
        low = lax.ppermute(
            lax.slice_in_dim(block, block.shape[dim] - width, None, axis=dim), axis, forward
        )
        high = lax.ppermute(lax.slice_in_dim(block, 0, width, axis=dim), axis, backward)
        block = jnp.concatenate([low, block, high], axis=dim)
    return block


def layer_norm(values):
    values = values.astype(jnp.float32)
    center = values - jnp.mean(values, axis=-1, keepdims=True)
    spread = jnp.mean(center * center, axis=-1, keepdims=True)
    return center * lax.rsqrt(spread + NORM_EPS)


def modulate(values, shift_row, scale_row):
    return layer_norm(values) * (1.0 + scale_row) + shift_row


def sigma_of(step_index, step_count):
    fraction = 1.0 - step_index.astype(jnp.float32) / step_count
    return SHIFT_FACTOR * fraction / (1.0 + (SHIFT_FACTOR - 1.0) * fraction)


def unpatchify(token_out, grid_width, patch_size, channels):
    patch_rows = token_out.shape[0] // grid_width
    shaped = token_out.reshape(patch_rows, grid_width, patch_size, patch_size, channels)
    shaped = jnp.transpose(shaped, (4, 0, 2, 1, 3))
    return shaped.reshape(channels, patch_rows * patch_size, grid_width * patch_size)


def convolve(padded, conv_w):
    row_count = padded.shape[1] - 2
    col_count = padded.shape[2] - 2
    tap_list = [
        padded[:, tap_row : tap_row + row_count, tap_col : tap_col + col_count]
        for tap_row in range(3)
        for tap_col in range(3)
    ]
    stacked = jnp.stack(tap_list, axis=1).reshape(padded.shape[0] * 9, row_count * col_count)
    convolved = jnp.dot(conv_w, stacked, preferred_element_type=jnp.float32)
    return convolved.reshape(conv_w.shape[0], row_count, col_count)


def text_state(queries, keys_txt, vals_txt, length):
    text_allowed = (jnp.arange(keys_txt.shape[0], dtype=jnp.int32) < length)[None, None, :]
    text_scores = (
        jnp.einsum("qhd,khd->qhk", queries, keys_txt, preferred_element_type=jnp.float32)
        * SCORE_SCALE
    )
    text_scores = jnp.where(text_allowed, text_scores, NEG_LARGE)
    text_max = jnp.max(text_scores, axis=2)
    text_weights = jnp.where(text_allowed, jnp.exp(text_scores - text_max[:, :, None]), 0.0)
    text_acc = jnp.einsum(
        "qhk,khd->qhd",
        text_weights.astype(jnp.bfloat16),
        vals_txt,
        preferred_element_type=jnp.float32,
    )
    return (text_max, jnp.sum(text_weights, axis=2), text_acc)


def absorb_block(previous, queries, head_keys, head_vals, allowed):
    old_max, old_sum, old_acc = previous
    scores = (
        jnp.einsum("qhd,khd->qhk", queries, head_keys, preferred_element_type=jnp.float32)
        * SCORE_SCALE
    )
    scores = jnp.where(allowed, scores, NEG_LARGE)
    new_max = jnp.maximum(old_max, jnp.max(scores, axis=2))
    weights = jnp.where(allowed, jnp.exp(scores - new_max[:, :, None]), 0.0)
    factor = jnp.exp(old_max - new_max)
    summed = jnp.einsum(
        "qhk,khd->qhd", weights.astype(jnp.bfloat16), head_vals, preferred_element_type=jnp.float32
    )
    return (
        new_max,
        old_sum * factor + jnp.sum(weights, axis=2),
        old_acc * factor[:, :, None] + summed,
    )


def absorb_maybe(previous, queries, head_keys, head_vals, allowed):
    return absorb_block(previous, queries, head_keys, head_vals, allowed)


def on_device(
    x_img,
    x_txt,
    modulation,
    w_img,
    w_txt,
    w_out,
    w_final,
    lengths,
    block_mask,
    timestep,
    latent,
    conv_w,
):
    tokens = x_img[0]
    factors = modulation[0]
    tok_rows = tokens.shape[0]
    head_cols = w_out.shape[0] * lax.axis_size("req")
    head_count = head_cols // HD
    h_img = modulate(tokens, factors[0], factors[1]).astype(jnp.bfloat16)
    h_txt = modulate(x_txt[0], factors[3], factors[4]).astype(jnp.bfloat16)
    qkv = jnp.dot(
        h_img, lax.all_gather(w_img, "req", axis=1, tiled=True), preferred_element_type=jnp.float32
    ).astype(jnp.bfloat16)
    kv_txt = jnp.dot(
        h_txt, lax.all_gather(w_txt, "req", axis=1, tiled=True), preferred_element_type=jnp.float32
    ).astype(jnp.bfloat16)
    keys_txt = kv_txt[:, :head_cols].reshape(-1, head_count, HD)
    vals_txt = kv_txt[:, head_cols:].reshape(-1, head_count, HD)
    length = lengths[0]
    queries = qkv[:, :head_cols].reshape(tok_rows, head_count, HD)
    keys_img = qkv[:, head_cols : 2 * head_cols]
    vals_img = qkv[:, 2 * head_cols :]
    mask_row = block_mask[0, 0]
    tile_count = mask_row.shape[0]
    start_state = text_state(queries, keys_txt, vals_txt, length)
    piece_keys = lax.all_gather(keys_img, "blk", axis=0, tiled=True)
    piece_vals = lax.all_gather(vals_img, "blk", axis=0, tiled=True)
    piece_len = piece_keys.shape[0]
    key_tile = jnp.arange(piece_len, dtype=jnp.int32) // tok_rows
    tile_hit = key_tile[:, None] == jnp.arange(tile_count, dtype=jnp.int32)[None, :]
    allowed = jnp.sum(jnp.where(tile_hit, mask_row[None, :], 0), axis=1) == 1
    head_keys = piece_keys.reshape(piece_len, head_count, HD)
    head_vals = piece_vals.reshape(piece_len, head_count, HD)
    run_max, run_sum, run_acc = absorb_maybe(
        start_state, queries, head_keys, head_vals, allowed[None, None, :]
    )
    attended = (run_acc / run_sum[:, :, None]).reshape(tok_rows, head_cols).astype(jnp.bfloat16)
    projected = jnp.dot(
        attended,
        lax.all_gather(w_out, "req", axis=0, tiled=True),
        preferred_element_type=jnp.float32,
    )
    residual = tokens.astype(jnp.float32) + factors[2] * projected
    final_in = modulate(residual, factors[5], factors[6]).astype(jnp.bfloat16)
    token_out = jnp.dot(final_in, w_final, preferred_element_type=jnp.float32)
    velocity = unpatchify(token_out, GRIDW, PATCH, LATC)[None]
    step_index = timestep[0]
    sigma_step = sigma_of(step_index + 1, NSTEPS) - sigma_of(step_index, NSTEPS)
    latent_next = latent + sigma_step * velocity
    decoded = (latent_next / LATENT_SCALE + LATENT_SHIFT).astype(jnp.bfloat16)
    padded = with_halo(decoded, (("blk", 2),), 1)
    padded = jnp.pad(padded[0], ((0, 0), (0, 0), (1, 1)))
    features = convolve(padded, conv_w).astype(jnp.bfloat16)[None]
    return (velocity, latent_next, features)


def solution(mesh):
    return jax.shard_map(
        on_device,
        mesh=mesh,
        in_specs=(
            P("req", "blk", None),
            P("req", None, None),
            P("req", None, None),
            P(None, "req"),
            P(None, "req"),
            P("req", None),
            P(),
            P("req"),
            P("req", "blk", None),
            P("req"),
            P("req", None, "blk", None),
            P(),
        ),
        out_specs=(
            P("req", None, "blk", None),
            P("req", None, "blk", None),
            P("req", None, "blk", None),
        ),
        check_vma=False,
    )
```

profile of v0, /device:TPU:0, one launch (start us, length us, event | category | flops | bytes accessed | tf_op | source)
XLA Modules:
  0.0 230.1 jit_solution(16971153236048344387)
XLA Ops:
  7.2 0.7 all-gather.8.cloned.1.call-update
  8.0 0.7 all-gather.6.cloned.1.call-update
  8.7 0.9 add_reduce_fusion
  9.6 0.2 convert_reduce_fusion
  9.8 0.3 fusion.14
  10.2 51.3 %all-gather.8.cloned.1.call-done = bf16[1536,2304]{0,1:T(8,128)(2,1)} async-done(((bf16[1536,288]{0,1:T(8,128)(2,1)}), bf16[1536,2304]{0,1:T(8,128)(2,1)}) %all-gather.8.cloned.1.call-update) | async-done | bytes 7077904 | tf_op jit(solution)/shard_map/all_gather | solution.py:132
  61.5 5.2 %convolution_convert_fusion = bf16[256,2304]{1,0:T(8,128)(2,1)S(1)} fusion(bf16[1536,2304]{0,1:T(8,128)(2,1)} %all-gather.8.cloned.1.call-done, bf16[1,256,1536]{2,1,0:T(8,128)(2,1)S(1)} %copy-done.2, f32[1536]{0:T(1024)S(1)} %get-tuple-element.16, f32[1536]{0:T(1024)S(1)} %get-tuple-element.17, f32[256]{0:T(256)S(1)} %add_rsqrt_fusion.1, ...), kind=kOutput, calls=%fused_computation.10 | convolution fusion | flops 1814888448 | bytes 9058304 | tf_op jit(solution)/shard_map/dot_general | solution.py:131
  66.7 1.0 fusion.69
  67.7 0.5 all-gather.12.cloned.1.call-update
  68.3 0.5 all-gather.14.cloned.1.call-update
  69.5 0.1 convert_reduce_fusion.1
  69.7 0.3 fusion.30
  70.7 0.1 select_reduce_fusion
  70.8 1.0 copy.66
  71.9 30.4 %all-gather.6.cloned.1.call-done = bf16[1536,1536]{0,1:T(8,128)(2,1)} async-done(((bf16[1536,192]{0,1:T(8,128)(2,1)}), bf16[1536,1536]{0,1:T(8,128)(2,1)}) %all-gather.6.cloned.1.call-update) | async-done | bytes 4718608 | tf_op jit(solution)/shard_map/all_gather | solution.py:135
  102.3 4.0 %convolution_convert_fusion.1 = bf16[154,1536]{1,0:T(8,128)(2,1)S(1)} fusion(bf16[1536,1536]{0,1:T(8,128)(2,1)} %all-gather.6.cloned.1.call-done, bf16[1,154,1536]{2,1,0:T(8,128)(2,1)S(1)} %copy-done.4, f32[1536]{0:T(1024)S(1)} %get-tuple-element.18, f32[1536]{0:T(1024)S(1)} %get-tuple-element.19, f32[154]{0:T(256)S(1)} %add_rsqrt_fusion.2, ...), kind=kOutput, calls=%fused_computation.13 | convolution fusion | flops 728318976 | bytes 5678288 | tf_op jit(solution)/shard_map/dot_general | solution.py:134
  106.4 0.9 copy.60
  107.3 0.9 copy.59
  108.3 0.2 copy.61
  108.4 1.6 bitcast_reduce_fusion.1
  110.0 0.6 fusion.18
  110.6 30.5 %all-gather.10.cloned.1.call-done = bf16[1024,768]{1,0:T(8,128)(2,1)} async-done(((bf16[256,768]{1,0:T(8,128)(2,1)}), bf16[1024,768]{1,0:T(8,128)(2,1)}) %all-gather.10.cloned.1.call-update) | async-done | bytes 1572880 | tf_op jit(solution)/shard_map/all_gather | solution.py:146
  141.0 2.6 %copy.62 = bf16[1024,768]{0,1:T(8,128)(2,1)} copy(bf16[1024,768]{1,0:T(8,128)(2,1)} %all-gather.10.cloned.1.call-done) | data formatting | bytes 3145728 | tf_op jit(solution)/shard_map/all_gather | solution.py:146
  143.6 8.8 %bitcast_reduce_fusion = (f32[256,12]{0,1:T(8,128)S(1)}, f32[12,1024,256]{2,1,0:T(8,128)}) fusion(pred[1024]{0:T(1024)(128)(4,1)S(1)} %broadcast_compare_fusion, bf16[1024,12,64]{0,2,1:T(8,128)(2,1)} %bitcast.129, bf16[256,12,64]{0,2,1:T(8,128)(2,1)S(1)} %bitcast.134), kind=kOutput, calls=%fused_computation.1 | convolution fusion | flops 412087296 | bytes 14562304 | tf_op jit(solution)/shard_map/qhd,khd->qhk/dot_general | solution.py:89
  152.5 26.0 %all-gather.12.cloned.1.call-done = bf16[1024,768]{1,0:T(8,128)(2,1)} async-done(((bf16[256,768]{1,0:T(8,128)(2,1)}), bf16[1024,768]{1,0:T(8,128)(2,1)}) %all-gather.12.cloned.1.call-update) | async-done | bytes 1572880 | tf_op jit(solution)/shard_map/all_gather | solution.py:147
  178.4 2.6 %copy.63 = bf16[1024,768]{0,1:T(8,128)(2,1)} copy(bf16[1024,768]{1,0:T(8,128)(2,1)} %all-gather.12.cloned.1.call-done) | data formatting | bytes 3145728 | tf_op jit(solution)/shard_map/all_gather | solution.py:147
  181.0 7.2 %fusion.2 = f32[256,12]{0,1:T(8,128)S(1)} fusion(f32[12,1024,256]{2,1,0:T(8,128)} %get-tuple-element.45, f32[256,12]{0,1:T(8,128)S(1)} %max.13, pred[1024]{0:T(1024)(128)(4,1)S(1)} %broadcast_compare_fusion), kind=kLoop, calls=%fused_computation.5 | loop fusion | flops 15725568 | bytes 12608512 | tf_op jit(solution)/shard_map/reduce_sum | solution.py:101
  188.3 1.3 copy-done.1
  189.6 4.3 %fusion.20 = f32[256,12,64]{0,2,1:T(8,128)S(1)} fusion(bf16[1024,12,64]{0,2,1:T(8,128)(2,1)} %bitcast.135, f32[12,1024,256]{2,1,0:T(8,128)S(1)} %copy-done.1, f32[256,12]{0,1:T(8,128)S(1)} %max.13, pred[1024]{0:T(1024)(128)(4,1)S(1)} %broadcast_compare_fusion), kind=kOutput, calls=%fused_computation.33 | convolution fusion | flops 418381824 | bytes 14955520 | tf_op jit(solution)/shard_map/qhk,khd->qhd/dot_general | solution.py:96
  193.9 0.7 fusion.26
  194.6 13.5 %all-gather.14.cloned.1.call-done = bf16[768,1536]{1,0:T(8,128)(2,1)} async-done(((bf16[96,1536]{1,0:T(8,128)(2,1)}), bf16[768,1536]{1,0:T(8,128)(2,1)}) %all-gather.14.cloned.1.call-update) | async-done | bytes 2359312 | tf_op jit(solution)/shard_map/all_gather | solution.py:160
  208.1 2.5 %fusion.72 = (f32[256]{0:T(256)S(1)}, f32[256,1536]{1,0:T(8,128)S(1)}) fusion(bf16[256,768]{0,1:T(8,128)(2,1)S(1)} %bitcast.137, bf16[768,1536]{1,0:T(8,128)(2,1)} %all-gather.14.cloned.1.call-done, f32[1536]{0:T(1024)S(1)} %get-tuple-element.20, bf16[1,256,1536]{2,1,0:T(8,128)(2,1)S(1)} %copy-done.2), kind=kOutput, calls=%fused_computation.127 | convolution fusion | flops 605552384 | bytes 5118976 | tf_op jit(solution)/shard_map/dot_general | solution.py:158
  210.6 0.3 multiply_reduce_fusion
  211.0 0.5 fusion.46
  211.4 0.1 reshape.190
  211.6 0.3 copy.65
  211.9 0.1 add_convert_fusion.2
  212.0 3.4 %collective-permute-start = (bf16[1,16,1,128]{1,3,2,0:T(8,128)(2,1)S(1)}, bf16[1,16,1,128]{1,3,2,0:T(8,128)(2,1)S(1)}, u32[]{:S(2)}, u32[]{:S(2)}) collective-permute-start(bf16[1,16,1,128]{1,3,2,0:T(8,128)(2,1)S(1)} %get-tuple-element.31), channel_id=1, source_target_pairs={{0,1},{1,2},{2,3},{4,5},{5,6},{6,7},{8,9},{9,10},{10,11},{12,13},{... | collective-permute-start | bytes 12296 | tf_op jit(solution)/shard_map/ppermute | solution.py:24
  215.4 1.3 collective-permute-start.1
  216.7 0.1 copy.68
  216.8 0.8 copy.79
  217.6 0.8 copy.80
  218.4 0.1 copy.67
  218.5 2.7 %collective-permute-done.1 = bf16[1,16,1,128]{1,3,2,0:T(8,128)(2,1)S(1)} collective-permute-done((bf16[1,16,1,128]{1,3,2,0:T(8,128)(2,1)S(1)}, bf16[1,16,1,128]{1,3,2,0:T(8,128)(2,1)S(1)}, u32[]{:S(2)}, u32[]{:S(2)}) %collective-permute-start.1) | collective-permute-done | bytes 4128 | tf_op jit(solution)/shard_map/ppermute | solution.py:27
  221.2 0.1 copy.69
  221.3 0.1 fusion.59
  221.6 0.5 convolution_convert_fusion.2
  222.1 1.5 copy.81
  (47 shorter events, 0.6 us)
Async XLA Ops:
  7.2 203.8 %copy-start = (bf16[1536,64]{0,1:T(8,128)(2,1)S(1)}, bf16[1536,64]{0,1:T(8,128)(2,1)}, u32[]{:S(2)}) copy-start(bf16[1536,64]{0,1:T(8,128)(2,1)} %param.18) | copy-start | bytes 589828
  7.2 2.5 %copy-start.2 = (bf16[1,256,1536]{2,1,0:T(8,128)(2,1)S(1)}, bf16[1,256,1536]{2,1,0:T(8,128)(2,1)}, u32[]{:S(2)}) copy-start(bf16[1,256,1536]{2,1,0:T(8,128)(2,1)} %param.12) | copy-start | bytes 2359300
  7.2 54.3 %all-gather.8.cloned.1.call-start = ((), (), s32[]{:S(2)}) async-start(), calls=%async_computation.1 | async-start | bytes 7962624 | tf_op jit(solution)/shard_map/all_gather | solution.py:132
  7.9 94.4 %all-gather.6.cloned.1.call-start = ((), (), s32[]{:S(2)}) async-start(), calls=%async_computation | async-start | bytes 5308416 | tf_op jit(solution)/shard_map/all_gather | solution.py:135
  8.7 132.4 %all-gather.10.cloned.1.call-start = ((), (), s32[]{:S(2)}) async-start(), calls=%async_computation.2 | async-start | bytes 1966080 | tf_op jit(solution)/shard_map/all_gather | solution.py:146
  66.7 2.9 %copy-start.4 = (bf16[1,154,1536]{2,1,0:T(8,128)(2,1)S(1)}, bf16[1,154,1536]{2,1,0:T(8,128)(2,1)}, u32[]{:S(2)}) copy-start(bf16[1,154,1536]{2,1,0:T(8,128)(2,1)} %param.13) | copy-start | bytes 1419268
  66.7 4.0 %copy-start.8 = (s32[1,1,4]{2,1,0:T(1,128)S(1)}, s32[1,1,4]{2,1,0:T(1,128)}, u32[]{:S(2)}) copy-start(s32[1,1,4]{2,1,0:T(1,128)} %param.20) | copy-start | bytes 52
  66.7 4.1 %copy-start.7 = (f32[1,16,8,128]{3,2,1,0:T(8,128)S(1)}, f32[1,16,8,128]{3,2,1,0:T(8,128)}, u32[]{:S(2)}) copy-start(f32[1,16,8,128]{3,2,1,0:T(8,128)} %param.22) | copy-start | bytes 196612
  67.7 110.8 %all-gather.12.cloned.1.call-start = ((), (), s32[]{:S(2)}) async-start(), calls=%async_computation.3 | async-start | bytes 1966080 | tf_op jit(solution)/shard_map/all_gather | solution.py:147
  68.3 139.8 %all-gather.14.cloned.1.call-start = ((), (), s32[]{:S(2)}) async-start(), calls=%async_computation.4 | async-start | bytes 2654208 | tf_op jit(solution)/shard_map/all_gather | solution.py:160
  181.0 8.5 %copy-start.1 = (f32[12,1024,256]{2,1,0:T(8,128)S(1)}, f32[12,1024,256]{2,1,0:T(8,128)}, u32[]{:S(2)}) copy-start(f32[12,1024,256]{2,1,0:T(8,128)} %get-tuple-element.45) | copy-start | bytes 37748740
  189.6 4.3 %copy-start.5 = (bf16[154,768]{0,1:T(8,128)(2,1)S(1)}, bf16[154,768]{0,1:T(8,128)(2,1)}, u32[]{:S(2)}) copy-start(bf16[154,768]{0,1:T(8,128)(2,1)} %copy.59) | copy-start | bytes 709636
  210.6 1.2 copy-start.3
  211.8 9.8 %copy-start.6 = (bf16[512,144]{0,1:T(8,128)(2,1)S(1)}, bf16[512,144]{0,1:T(8,128)(2,1)}, u32[]{:S(2)}) copy-start(bf16[512,144]{0,1:T(8,128)(2,1)} %param.23) | copy-start | bytes 442372
  212.0 6.4 %collective-permute-start = (bf16[1,16,1,128]{1,3,2,0:T(8,128)(2,1)S(1)}, bf16[1,16,1,128]{1,3,2,0:T(8,128)(2,1)S(1)}, u32[]{:S(2)}, u32[]{:S(2)}) collective-permute-start(bf16[1,16,1,128]{1,3,2,0:T(8,128)(2,1)S(1)} %get-tuple-element.31), channel_id=1, source_target_pairs={{0,1},{1,2},{2,3},{4,5},{5,6},{6,7},{8,9},{9,10},{10,11},{12,13},{... | collective-permute-start | bytes 12296 | tf_op jit(solution)/shard_map/ppermute | solution.py:24
  215.4 5.8 %collective-permute-start.1 = (bf16[1,16,1,128]{1,3,2,0:T(8,128)(2,1)S(1)}, bf16[1,16,1,128]{1,3,2,0:T(8,128)(2,1)S(1)}, u32[]{:S(2)}, u32[]{:S(2)}) collective-permute-start(bf16[1,16,1,128]{1,3,2,0:T(8,128)(2,1)S(1)} %get-tuple-element.32), channel_id=1, source_target_pairs={{1,0},{2,1},{3,2},{5,4},{6,5},{7,6},{9,8},{10,9},{11,10},{13,12},{... | collective-permute-start | bytes 12296 | tf_op jit(solution)/shard_map/ppermute | solution.py:27
Sparse Core Ops, SparseCore 0:
  9.9 51.5 all-gather.7
  63.4 38.9 all-gather.5
  103.9 37.0 all-gather.9
  142.5 35.9 all-gather.11
  180.2 27.8 all-gather.13
where the time goes:
time: 231 us; the launch traced here: 230 us
  waiting for transfers between devices  157 us (68%)
  matrix products  28 us (12%)
  between operations  15.5 us (7%)
  local copies, waits for them, and re-layouts  14.5 us (6%)
  other arithmetic  10.2 us (4%)
  starting transfers between devices  4.88 us (2%)
    all_gather x1, waiting for transfers between devices, on_device(): lax.all_gather(w_img, 'req', axis=1, tiled=True)  51.3 us
    all_gather x1, waiting for transfers between devices, on_device(): piece_keys = lax.all_gather(keys_img, 'blk', axis=0, tiled=True)  30.5 us
    all_gather x1, waiting for transfers between devices, on_device(): lax.all_gather(w_txt, 'req', axis=1, tiled=True)  30.4 us
    all_gather x1, waiting for transfers between devices, on_device(): piece_vals = lax.all_gather(vals_img, 'blk', axis=0, tiled=True)  26 us
    all_gather x1, waiting for transfers between devices, on_device(): lax.all_gather(w_out, 'req', axis=0, tiled=True)  13.5 us
    dot_general x1, matrix products, absorb_block(): jnp.einsum('qhd,khd->qhk', queries, head_keys, preferred_element_type=jnp...  8.82 us
    reduce_sum x1, other arithmetic, absorb_block(): jnp.sum(weights, axis=2)  7.21 us
    unnamed x30, local copies, waits for them, and re-layouts  5.57 us
  transfers between devices with their start and end apart: 7, of which 6 were waited for; matrix products, arithmetic and copies ran while one was open for 20% of the time, Pallas kernels for 0%

commit v1 on v0

--- a/solution.py
+++ b/solution.py
@@ -143,8 +143,13 @@
     mask_row = block_mask[0, 0]
     tile_count = mask_row.shape[0]
     start_state = text_state(queries, keys_txt, vals_txt, length)
-    piece_keys = lax.all_gather(keys_img, "blk", axis=0, tiled=True)
-    piece_vals = lax.all_gather(vals_img, "blk", axis=0, tiled=True)
+    piece_keys, piece_vals = jnp.split(
+        jax.lax.all_gather(
+            jnp.concatenate([keys_img, vals_img], axis=1), axis_name="blk", axis=0, tiled=True
+        ),
+        [keys_img.shape[1]],
+        axis=1,
+    )
     piece_len = piece_keys.shape[0]
     key_tile = jnp.arange(piece_len, dtype=jnp.int32) // tok_rows
     tile_hit = key_tile[:, None] == jnp.arange(tile_count, dtype=jnp.int32)[None, :]

time: 231 us -> 220 us (0.952)
  waiting for transfers between devices: 157 us -> 145 us
  local copies, waits for them, and re-layouts: 14.5 us -> 18.3 us
    all_gather x1, waiting for transfers between devices: 13.5 us -> 0.02 us  [on_device(): lax.all_gather(w_out, 'req', axis=0, tiled=True)]
    split x0 -> x3, local copies, waits for them, and re-layouts: none -> 8.96 us  [on_device(): jnp.split(jax.lax.all_gather(jnp.concatenate([keys_img, vals_img], axis=1...]
    all_gather x2 -> x0, local copies, waits for them, and re-layouts: 5.2 us -> none  [the longest x1 2.6 us: on_device(): piece_keys = lax.all_gather(keys_img, 'blk', axis=0, tiled=True)]
    all_gather x2 -> x1, waiting for transfers between devices: 56.5 us -> 57.4 us  [on_device(): jax.lax.all_gather(jnp.concatenate([keys_img, vals_img], axis=1), axis_na...]
  transfers between devices with their start and end apart: 7 -> 6, of which waited for: 6 -> 4; matrix products, arithmetic and copies ran while one was open for 20% -> 22% of each run, Pallas kernels for 0% -> 0%
where the time goes in v1:
time: 220 us
  waiting for transfers between devices  145 us (66%)
  matrix products  28.1 us (13%)
  local copies, waits for them, and re-layouts  18.3 us (8%)
  between operations  15.5 us (7%)
  other arithmetic  10.4 us (5%)
  starting transfers between devices  2.74 us (1%)
    all_gather x1, waiting for transfers between devices, on_device(): jax.lax.all_gather(jnp.concatenate([keys_img, vals_img], axis=1), axis_na...  57.4 us
    all_gather x1, waiting for transfers between devices, on_device(): lax.all_gather(w_img, 'req', axis=1, tiled=True)  51.3 us
    all_gather x1, waiting for transfers between devices, on_device(): lax.all_gather(w_txt, 'req', axis=1, tiled=True)  31.1 us
    split x3, local copies, waits for them, and re-layouts, on_device(): jnp.split(jax.lax.all_gather(jnp.concatenate([keys_img, vals_img], axis=1...  8.96 us
    dot_general x1, matrix products, absorb_block(): jnp.einsum('qhd,khd->qhk', queries, head_keys, preferred_element_type=jnp...  8.88 us
    reduce_sum x1, other arithmetic, absorb_block(): jnp.sum(weights, axis=2)  7.42 us
    unnamed x30, local copies, waits for them, and re-layouts  5.58 us
    dot_general x1, matrix products, on_device(): jnp.dot(h_img, lax.all_gather(w_img, 'req', axis=1, tiled=True), preferre...  5.16 us
  transfers between devices with their start and end apart: 6, of which 4 were waited for; matrix products, arithmetic and copies ran while one was open for 22% of the time, Pallas kernels for 0%

profile of v1, /device:TPU:0, one launch (start us, length us, event | category | flops | bytes accessed | tf_op | source)
XLA Modules:
  0.0 219.7 jit_solution(10724856641224826074)
XLA Ops:
  7.2 0.7 all-gather.7.cloned.1.call-update
  8.0 0.7 all-gather.5.cloned.1.call-update
  8.7 0.0 all-gather.9.cloned.1.call-start
  8.7 0.9 add_reduce_fusion
  9.6 0.2 convert_reduce_fusion
  9.8 0.3 fusion.14
  10.2 51.3 %all-gather.7.cloned.1.call-done = bf16[1536,2304]{0,1:T(8,128)(2,1)} async-done(((bf16[1536,288]{0,1:T(8,128)(2,1)}), bf16[1536,2304]{0,1:T(8,128)(2,1)}) %all-gather.7.cloned.1.call-update) | async-done | bytes 7077904 | tf_op jit(solution)/shard_map/all_gather | solution.py:132
  61.5 5.2 %convolution_convert_fusion = bf16[256,2304]{1,0:T(8,128)(2,1)S(1)} fusion(bf16[1536,2304]{0,1:T(8,128)(2,1)} %all-gather.7.cloned.1.call-done, bf16[1,256,1536]{2,1,0:T(8,128)(2,1)S(1)} %copy-done.2, f32[1536]{0:T(1024)S(1)} %get-tuple-element.16, f32[1536]{0:T(1024)S(1)} %get-tuple-element.17, f32[256]{0:T(256)S(1)} %add_rsqrt_fusion.1, ...), kind=kOutput, calls=%fused_computation.10 | convolution fusion | flops 1814888448 | bytes 9058304 | tf_op jit(solution)/shard_map/dot_general | solution.py:131
  66.7 0.9 concatenate.8
  67.7 0.0 all-gather.11.cloned.1.call-start
  67.7 0.5 all-gather.11.cloned.1.call-update
  68.9 0.1 convert_reduce_fusion.1
  69.1 0.3 fusion.30
  70.0 0.1 select_reduce_fusion
  70.2 1.0 copy.66
  71.3 31.1 %all-gather.5.cloned.1.call-done = bf16[1536,1536]{0,1:T(8,128)(2,1)} async-done(((bf16[1536,192]{0,1:T(8,128)(2,1)}), bf16[1536,1536]{0,1:T(8,128)(2,1)}) %all-gather.5.cloned.1.call-update) | async-done | bytes 4718608 | tf_op jit(solution)/shard_map/all_gather | solution.py:135
  102.4 4.0 %convolution_convert_fusion.1 = bf16[154,1536]{1,0:T(8,128)(2,1)S(1)} fusion(bf16[1536,1536]{0,1:T(8,128)(2,1)} %all-gather.5.cloned.1.call-done, bf16[1,154,1536]{2,1,0:T(8,128)(2,1)S(1)} %copy-done.4, f32[1536]{0:T(1024)S(1)} %get-tuple-element.18, f32[1536]{0:T(1024)S(1)} %get-tuple-element.19, f32[154]{0:T(256)S(1)} %add_rsqrt_fusion.2, ...), kind=kOutput, calls=%fused_computation.13 | convolution fusion | flops 728318976 | bytes 5678288 | tf_op jit(solution)/shard_map/dot_general | solution.py:134
  106.4 0.9 copy.60
  107.4 0.9 copy.59
  108.3 0.2 copy.61
  108.5 1.6 bitcast_reduce_fusion.1
  110.0 0.6 fusion.18
  110.6 57.4 %all-gather.9.cloned.1.call-done = bf16[1024,1536]{1,0:T(8,128)(2,1)} async-done(((bf16[256,1536]{1,0:T(8,128)(2,1)}), bf16[1024,1536]{1,0:T(8,128)(2,1)}) %all-gather.9.cloned.1.call-update) | async-done | bytes 3145744 | tf_op jit(solution)/shard_map/all_gather | solution.py:147
  168.0 3.8 %fusion.69 = (bf16[1024,768]{1,0:T(8,128)(2,1)}, bf16[1024,768]{1,0:T(8,128)(2,1)}) fusion(bf16[1024,1536]{1,0:T(8,128)(2,1)} %all-gather.9.cloned.1.call-done), kind=kLoop, calls=%fused_computation.124 | loop fusion | bytes 6291456 | tf_op jit(solution)/shard_map/split | solution.py:146
  171.8 2.6 %copy.62 = bf16[1024,768]{0,1:T(8,128)(2,1)} copy(bf16[1024,768]{1,0:T(8,128)(2,1)} %get-tuple-element.26) | data formatting | bytes 3145728 | tf_op jit(solution)/shard_map/split | solution.py:146
  174.4 8.9 %bitcast_reduce_fusion = (f32[256,12]{0,1:T(8,128)S(1)}, f32[12,1024,256]{2,1,0:T(8,128)}) fusion(pred[1024]{0:T(1024)(128)(4,1)S(1)} %broadcast_compare_fusion, bf16[1024,12,64]{0,2,1:T(8,128)(2,1)} %bitcast.129, bf16[256,12,64]{0,2,1:T(8,128)(2,1)S(1)} %bitcast.134), kind=kOutput, calls=%fused_computation.1 | convolution fusion | flops 412087296 | bytes 14562304 | tf_op jit(solution)/shard_map/qhd,khd->qhk/dot_general | solution.py:89
  183.3 2.6 %copy.63 = bf16[1024,768]{0,1:T(8,128)(2,1)} copy(bf16[1024,768]{1,0:T(8,128)(2,1)} %get-tuple-element.27) | data formatting | bytes 3145728 | tf_op jit(solution)/shard_map/split | solution.py:146
  185.9 7.4 %fusion.2 = f32[256,12]{0,1:T(8,128)S(1)} fusion(f32[12,1024,256]{2,1,0:T(8,128)} %get-tuple-element.44, f32[256,12]{0,1:T(8,128)S(1)} %max.13, pred[1024]{0:T(1024)(128)(4,1)S(1)} %broadcast_compare_fusion), kind=kLoop, calls=%fused_computation.5 | loop fusion | flops 15725568 | bytes 12608512 | tf_op jit(solution)/shard_map/reduce_sum | solution.py:101
  193.3 1.3 copy-done.1
  194.6 4.3 %fusion.20 = f32[256,12,64]{0,2,1:T(8,128)S(1)} fusion(bf16[1024,12,64]{0,2,1:T(8,128)(2,1)} %bitcast.135, f32[12,1024,256]{2,1,0:T(8,128)S(1)} %copy-done.1, f32[256,12]{0,1:T(8,128)S(1)} %max.13, pred[1024]{0:T(1024)(128)(4,1)S(1)} %broadcast_compare_fusion), kind=kOutput, calls=%fused_computation.33 | convolution fusion | flops 418381824 | bytes 14955520 | tf_op jit(solution)/shard_map/qhk,khd->qhd/dot_general | solution.py:96
  199.0 0.7 fusion.26
  199.6 2.5 %fusion.72 = (f32[256]{0:T(256)S(1)}, f32[256,1536]{1,0:T(8,128)S(1)}) fusion(bf16[256,768]{0,1:T(8,128)(2,1)S(1)} %bitcast.137, bf16[768,1536]{1,0:T(8,128)(2,1)} %all-gather.11.cloned.1.call-done, f32[1536]{0:T(1024)S(1)} %get-tuple-element.20, bf16[1,256,1536]{2,1,0:T(8,128)(2,1)S(1)} %copy-done.2), kind=kOutput, calls=%fused_computation.127 | convolution fusion | flops 605552384 | bytes 5118976 | tf_op jit(solution)/shard_map/dot_general | solution.py:163
  202.2 0.3 multiply_reduce_fusion
  202.5 0.5 fusion.46
  203.0 0.1 reshape.190
  203.1 0.3 copy.65
  203.4 0.1 add_convert_fusion.2
  203.5 1.3 collective-permute-start
  204.8 1.3 collective-permute-start.1
  206.1 0.1 copy.68
  206.3 0.8 copy.79
  207.1 0.8 copy.80
  207.9 0.1 copy.67
  207.9 2.8 %collective-permute-done.1 = bf16[1,16,1,128]{1,3,2,0:T(8,128)(2,1)S(1)} collective-permute-done((bf16[1,16,1,128]{1,3,2,0:T(8,128)(2,1)S(1)}, bf16[1,16,1,128]{1,3,2,0:T(8,128)(2,1)S(1)}, u32[]{:S(2)}, u32[]{:S(2)}) %collective-permute-start.1) | collective-permute-done | bytes 4128 | tf_op jit(solution)/shard_map/ppermute | solution.py:27
  210.8 0.1 copy.69
  210.9 0.1 fusion.59
  211.2 0.5 convolution_convert_fusion.2
  211.7 1.5 copy.81
  (46 shorter events, 0.5 us)
Async XLA Ops:
  7.2 195.4 %copy-start = (bf16[1536,64]{0,1:T(8,128)(2,1)S(1)}, bf16[1536,64]{0,1:T(8,128)(2,1)}, u32[]{:S(2)}) copy-start(bf16[1536,64]{0,1:T(8,128)(2,1)} %param.18) | copy-start | bytes 589828
  7.2 2.5 %copy-start.2 = (bf16[1,256,1536]{2,1,0:T(8,128)(2,1)S(1)}, bf16[1,256,1536]{2,1,0:T(8,128)(2,1)}, u32[]{:S(2)}) copy-start(bf16[1,256,1536]{2,1,0:T(8,128)(2,1)} %param.12) | copy-start | bytes 2359300
  7.2 54.3 %all-gather.7.cloned.1.call-start = ((), (), s32[]{:S(2)}) async-start(), calls=%async_computation.1 | async-start | bytes 7962624 | tf_op jit(solution)/shard_map/all_gather | solution.py:132
  7.9 94.4 %all-gather.5.cloned.1.call-start = ((), (), s32[]{:S(2)}) async-start(), calls=%async_computation | async-start | bytes 5308416 | tf_op jit(solution)/shard_map/all_gather | solution.py:135
  8.7 159.4 %all-gather.9.cloned.1.call-start = ((), (), s32[]{:S(2)}) async-start(), calls=%async_computation.2 | async-start | bytes 3932160 | tf_op jit(solution)/shard_map/all_gather | solution.py:147
  66.7 2.2 %copy-start.4 = (bf16[1,154,1536]{2,1,0:T(8,128)(2,1)S(1)}, bf16[1,154,1536]{2,1,0:T(8,128)(2,1)}, u32[]{:S(2)}) copy-start(bf16[1,154,1536]{2,1,0:T(8,128)(2,1)} %param.13) | copy-start | bytes 1419268
  66.7 3.4 %copy-start.8 = (s32[1,1,4]{2,1,0:T(1,128)S(1)}, s32[1,1,4]{2,1,0:T(1,128)}, u32[]{:S(2)}) copy-start(s32[1,1,4]{2,1,0:T(1,128)} %param.20) | copy-start | bytes 52
  66.7 3.5 %copy-start.7 = (f32[1,16,8,128]{3,2,1,0:T(8,128)S(1)}, f32[1,16,8,128]{3,2,1,0:T(8,128)}, u32[]{:S(2)}) copy-start(f32[1,16,8,128]{3,2,1,0:T(8,128)} %param.22) | copy-start | bytes 196612
  67.7 132.0 %all-gather.11.cloned.1.call-start = ((), (), s32[]{:S(2)}) async-start(), calls=%async_computation.3 | async-start | bytes 2654208 | tf_op jit(solution)/shard_map/all_gather | solution.py:165
  185.9 8.7 %copy-start.1 = (f32[12,1024,256]{2,1,0:T(8,128)S(1)}, f32[12,1024,256]{2,1,0:T(8,128)}, u32[]{:S(2)}) copy-start(f32[12,1024,256]{2,1,0:T(8,128)} %get-tuple-element.44) | copy-start | bytes 37748740
  194.6 4.3 %copy-start.5 = (bf16[154,768]{0,1:T(8,128)(2,1)S(1)}, bf16[154,768]{0,1:T(8,128)(2,1)}, u32[]{:S(2)}) copy-start(bf16[154,768]{0,1:T(8,128)(2,1)} %copy.59) | copy-start | bytes 709636
  202.2 1.2 copy-start.3
  203.4 7.8 %copy-start.6 = (bf16[512,144]{0,1:T(8,128)(2,1)S(1)}, bf16[512,144]{0,1:T(8,128)(2,1)}, u32[]{:S(2)}) copy-start(bf16[512,144]{0,1:T(8,128)(2,1)} %param.23) | copy-start | bytes 442372
  203.5 4.3 %collective-permute-start = (bf16[1,16,1,128]{1,3,2,0:T(8,128)(2,1)S(1)}, bf16[1,16,1,128]{1,3,2,0:T(8,128)(2,1)S(1)}, u32[]{:S(2)}, u32[]{:S(2)}) collective-permute-start(bf16[1,16,1,128]{1,3,2,0:T(8,128)(2,1)S(1)} %get-tuple-element.30), channel_id=1, source_target_pairs={{0,1},{1,2},{2,3},{4,5},{5,6},{6,7},{8,9},{9,10},{10,11},{12,13},{... | collective-permute-start | bytes 12296 | tf_op jit(solution)/shard_map/ppermute | solution.py:24
  204.8 5.9 %collective-permute-start.1 = (bf16[1,16,1,128]{1,3,2,0:T(8,128)(2,1)S(1)}, bf16[1,16,1,128]{1,3,2,0:T(8,128)(2,1)S(1)}, u32[]{:S(2)}, u32[]{:S(2)}) collective-permute-start(bf16[1,16,1,128]{1,3,2,0:T(8,128)(2,1)S(1)} %get-tuple-element.31), channel_id=1, source_target_pairs={{1,0},{2,1},{3,2},{5,4},{6,5},{7,6},{9,8},{10,9},{11,10},{13,12},{... | collective-permute-start | bytes 12296 | tf_op jit(solution)/shard_map/ppermute | solution.py:27
Sparse Core Ops, SparseCore 0:
  9.9 51.5 all-gather.6
  63.4 38.9 all-gather.4
  104.5 63.4 all-gather.8
  169.8 27.6 all-gather.10
